TPU v7x, 128 devices: a whole 4x4x4 slice. The times are simulated.
128 devices in a mesh: row: 16 (over z_lo, y, core), cand: 8 (over z_hi, x).
Axes of the slice: x: 4, y: 4, z: 4 (z_hi: 2, z_lo: 2; z = z_hi * 2 + z_lo), core: 2. Of those that a mesh axis runs over, the one named last changes fastest.
Arguments:
- embeddings: bfloat16 [131072, 768], P('row')
- pick_index: int32 [64], replicated, may hold values from 0 to 131071
- cand_index: int32 [8192], replicated, may hold values from 0 to 131071
Outputs:
- gains: float32 [8192], P('cand')
- coverage: float32 [131072], P('row')
All inputs are finite; a program needn't handle non-finite values.
Results may differ from a plain program's by a relative error of at most 0.0003.
Values may be sent and summed in bfloat16 or wider, within the bound.
A program may use at most 128 MiB of HBM per device.

v0:
```python
import jax
import jax.numpy as jnp
from jax import lax
from jax.sharding import PartitionSpec as P


def select_owned(embeddings, indices):
    count = embeddings.shape[0]
    local = indices - lax.axis_index("row") * count
    owned = (local >= 0) & (local < count)
    taken = jnp.take(embeddings, jnp.clip(local, 0, count - 1), axis=0)
    return jnp.where(owned[:, None], taken, jnp.zeros_like(taken))


def inner(left, right):
    return lax.dot_general(
        left, right, (((1,), (1,)), ((), ())), preferred_element_type=jnp.float32
    )


def per_device(embeddings, pick_index, cand_index):
    count = embeddings.shape[0]
    picked = (
        lax.psum(select_owned(embeddings, pick_index), "row")
        .astype(jnp.float32)
        .astype(jnp.bfloat16)
    )
    coverage = jnp.max(inner(embeddings, picked), axis=1)
    per_column = cand_index.shape[0] // lax.axis_size("cand")
    every = (
        lax.psum(select_owned(embeddings, cand_index), "row")
        .astype(jnp.float32)
        .astype(jnp.bfloat16)
    )
    chosen = lax.dynamic_slice_in_dim(every, lax.axis_index("cand") * per_column, per_column, 0)
    similar = inner(embeddings, chosen)
    partial_gain = jnp.sum(jnp.maximum(similar - coverage[:, None], 0.0), axis=0)
    total_rows = count * lax.axis_size("row")
    gains = lax.psum(partial_gain, "row") / total_rows
    return (gains, coverage)


def solution(mesh):
    return jax.shard_map(
        per_device,
        mesh=mesh,
        in_specs=(P("row", None), P(), P()),
        out_specs=(P("cand"), P("row")),
        check_vma=False,
    )
```

profile of v0, /device:TPU:0, one launch (start us, length us, event | category | flops | bytes accessed | tf_op | source)
XLA Modules:
  0.0 298.8 jit_solution(3463207593277725131)
XLA Ops:
  7.2 0.0 all-reduce.3.cloned.1.call-start
  7.2 0.8 compare_and_fusion.1
  8.0 0.8 fusion.1
  8.8 0.7 compare_and_fusion.2
  9.5 7.0 %gather_fusion.1 = bf16[64,768]{1,0:T(8,128)(2,1)S(1)} fusion(bf16[8192,768]{1,0:T(8,128)(2,1)} %param.3, s32[1024]{0:T(1024)S(1)} %pad_clamp_fusion), kind=kCustom, calls=%fused_computation.1 | custom fusion | bytes 196864 | tf_op jit(solution)/shard_map/jit(_take)/gather | solution.py:11
  16.4 43.3 %gather_fusion = bf16[8192,768]{1,0:T(8,128)(2,1)} fusion(bf16[8192,768]{1,0:T(8,128)(2,1)} %param.3, s32[8192]{0:T(1024)S(1)} %fusion.1), kind=kCustom, calls=%fused_computation | custom fusion | bytes 25198592 | tf_op jit(solution)/shard_map/jit(_take)/gather | solution.py:11
  59.7 0.7 select_select_fusion.1
  60.4 13.0 %select_select_fusion = bf16[8192,768]{1,0:T(8,128)(2,1)} fusion(bf16[8192,768]{1,0:T(8,128)(2,1)} %gather_fusion, pred[8192]{0:T(1024)(128)(4,1)S(1)} %get-tuple-element.7, pred[8192]{0:T(1024)(128)(4,1)S(1)} %get-tuple-element.6), kind=kLoop, calls=%fused_computation.3 | loop fusion | flops 12582912 | bytes 25182208 | tf_op jit(solution)/shard_map/jit(_where)/select_n | solution.py:12
  73.5 0.0 all-reduce.3.cloned.1.call-update
  73.5 163.0 %all-reduce.3.cloned.1.call-done = (bf16[64,768]{1,0:T(8,128)(2,1)}, bf16[8192,768]{1,0:T(8,128)(2,1)}) async-done(((bf16[64,768]{1,0:T(8,128)(2,1)}, bf16[8192,768]{1,0:T(8,128)(2,1)}), (bf16[64,768]{1,0:T(8,128)(2,1)}, bf16[8192,768]{1,0:T(8,128)(2,1)})) %all-reduce.3.cloned.1.call-update) | async-done | bytes 12681232 | tf_op jit(solution)/shard_map/psum | solution.py:24
  236.4 8.5 %convolution_reduce_fusion = f32[8192]{0:T(1024)S(1)} fusion(bf16[64,768]{1,0:T(8,128)(2,1)} %get-tuple-element.2, bf16[8192,768]{1,0:T(8,128)(2,1)} %param.3), kind=kOutput, calls=%fused_computation.5 | convolution fusion | flops 805822464 | bytes 12713984 | tf_op jit(solution)/shard_map/dot_general | solution.py:16
  245.0 0.0 copy-start
  245.0 16.8 %maximum_reduce_fusion = f32[1024]{0:T(1024)S(1)} fusion(bf16[8192,768]{1,0:T(8,128)(2,1)} %param.3, f32[8192]{0:T(1024)S(1)} %convolution_reduce_fusion, bf16[8192,768]{1,0:T(8,128)(2,1)} %get-tuple-element.3, s32[]{:T(128)S(6)} %select_n.32), kind=kOutput, calls=%fused_computation.2 | convolution fusion | flops 12910066688 | bytes 14192644 | tf_op jit(solution)/shard_map/dot_general | solution.py:16
  261.8 0.0 copy-done
  261.8 29.5 %psum.23 = f32[1024]{0:T(1024)S(1)} all-reduce(f32[1024]{0:T(1024)S(1)} %maximum_reduce_fusion), channel_id=1, replica_groups=mesh['row'=16,'cand'=8] {'row'}, use_global_device_ids=true, to_apply=%region_4.5 | all-reduce | flops 1024 | bytes 8192 | tf_op jit(solution)/shard_map/psum | solution.py:39
  291.3 0.6 broadcast_multiply_fusion
  (1 shorter events, 0.0 us)
Async XLA Ops:
  7.2 229.3 %all-reduce.3.cloned.1.call-start = ((), (), s32[]{:S(2)}) async-start(), calls=%async_computation | async-start | bytes 25362432 | tf_op jit(solution)/shard_map/psum | solution.py:24
  245.0 16.8 %copy-start = (f32[8192]{0:T(1024)}, f32[8192]{0:T(1024)S(1)}, u32[]{:S(2)}) copy-start(f32[8192]{0:T(1024)S(1)} %convolution_reduce_fusion) | copy-start | bytes 98308
Sparse Core Ops, SparseCore 0:
  73.6 162.8 all-reduce.2
where the time goes:
time: 299 us
  waiting for transfers between devices  163 us (55%)
  local copies, waits for them, and re-layouts  50.2 us (17%)
  blocking collectives  29.5 us (10%)
  matrix products  25.3 us (8%)
  other arithmetic  16.6 us (6%)
  between operations  14.1 us (5%)
    psum x1, waiting for transfers between devices, per_device(): lax.psum(select_owned(embeddings, pick_index), 'row').astype(jnp.float32)  163 us
    gather x2, local copies, waits for them, and re-layouts, select_owned(): taken = jnp.take(embeddings, jnp.clip(local, 0, count - 1), axis=0)  50.2 us
    psum x1, blocking collectives, per_device(): gains = lax.psum(partial_gain, 'row') / total_rows  29.5 us
    dot_general x2, matrix products, inner(): lax.dot_general(left, right, (((1,), (1,)), ((), ())), preferred_element_...  25.3 us
    select_n x2, other arithmetic, select_owned(): return jnp.where(owned[:, None], taken, jnp.zeros_like(taken))  13.8 us
  transfers between devices with their start and end apart: 1, of which 1 were waited for; matrix products, arithmetic and copies ran while one was open for 0% of the time, Pallas kernels for 0%

commit v1 on v0

--- a/solution.py
+++ b/solution.py
@@ -21,7 +21,7 @@
 def per_device(embeddings, pick_index, cand_index):
     count = embeddings.shape[0]
     picked = (
-        lax.psum(select_owned(embeddings, pick_index), "row")
+        jnp.sum(lax.all_gather(select_owned(embeddings, pick_index), "row"), axis=0)
         .astype(jnp.float32)
         .astype(jnp.bfloat16)
     )

time: 299 us -> 288 us (0.963)
  waiting for transfers between devices: 163 us -> 152 us
    psum x1, waiting for transfers between devices: 163 us -> 151 us  [per_device(): lax.psum(select_owned(embeddings, cand_index), 'row').astype(jnp.float32)]
  transfers between devices with their start and end apart: 1 -> 2, of which waited for: 1 -> 1; matrix products, arithmetic and copies ran while one was open for 0% -> 23% of each run, Pallas kernels for 0% -> 0%
where the time goes in v1:
time: 288 us
  waiting for transfers between devices  152 us (53%)
  local copies, waits for them, and re-layouts  50.2 us (17%)
  blocking collectives  29.4 us (10%)
  matrix products  25.3 us (9%)
  other arithmetic  17.5 us (6%)
  between operations  14.1 us (5%)
    psum x1, waiting for transfers between devices, per_device(): lax.psum(select_owned(embeddings, cand_index), 'row').astype(jnp.float32)  151 us
    gather x2, local copies, waits for them, and re-layouts, select_owned(): taken = jnp.take(embeddings, jnp.clip(local, 0, count - 1), axis=0)  50.2 us
    psum x1, blocking collectives, per_device(): gains = lax.psum(partial_gain, 'row') / total_rows  29.4 us
    dot_general x2, matrix products, inner(): lax.dot_general(left, right, (((1,), (1,)), ((), ())), preferred_element_...  25.3 us
    select_n x2, other arithmetic, select_owned(): return jnp.where(owned[:, None], taken, jnp.zeros_like(taken))  13.8 us
  transfers between devices with their start and end apart: 2, of which 1 were waited for; matrix products, arithmetic and copies ran while one was open for 23% of the time, Pallas kernels for 0%

profile of v1, /device:TPU:0, one launch (start us, length us, event | category | flops | bytes accessed | tf_op | source)
XLA Modules:
  0.0 288.1 jit_solution(3860313337172095971)
XLA Ops:
  7.2 0.0 all-gather.2.cloned.1.call-start
  7.2 0.7 compare_and_fusion.2
  7.9 7.0 %gather_fusion.1 = bf16[64,768]{1,0:T(8,128)(2,1)S(1)} fusion(bf16[8192,768]{1,0:T(8,128)(2,1)} %param.3, s32[1024]{0:T(1024)S(1)} %pad_clamp_fusion), kind=kCustom, calls=%fused_computation.1 | custom fusion | bytes 196864 | tf_op jit(solution)/shard_map/jit(_take)/gather | solution.py:11
  14.9 0.7 fusion.1
  15.6 0.0 all-gather.2.cloned.1.call-update
  15.6 0.0 all-reduce.2.cloned.1.call-start
  15.6 0.8 fusion.2
  16.4 0.0 copy-start
  16.4 43.3 %gather_fusion = bf16[8192,768]{1,0:T(8,128)(2,1)} fusion(bf16[8192,768]{1,0:T(8,128)(2,1)} %param.3, s32[8192]{0:T(1024)S(1)} %fusion.2), kind=kCustom, calls=%fused_computation | custom fusion | bytes 25198592 | tf_op jit(solution)/shard_map/jit(_take)/gather | solution.py:11
  59.7 0.0 copy-done
  59.7 13.1 %select_select_fusion = bf16[8192,768]{1,0:T(8,128)(2,1)} fusion(bf16[8192,768]{1,0:T(8,128)(2,1)} %gather_fusion, pred[8192]{0:T(1024)(128)(4,1)S(1)} %get-tuple-element.5, pred[8192]{0:T(1024)(128)(4,1)S(1)} %get-tuple-element.4), kind=kLoop, calls=%fused_computation.3 | loop fusion | flops 12582912 | bytes 25182208 | tf_op jit(solution)/shard_map/jit(_where)/select_n | solution.py:12
  72.8 0.0 all-reduce.2.cloned.1.call-update
  72.8 0.0 all-gather.2.cloned.1.call-done
  72.8 1.6 reduce_sum.21
  74.5 8.5 %convolution_reduce_fusion = f32[8192]{0:T(1024)S(1)} fusion(bf16[64,768]{1,0:T(8,128)(2,1)S(1)} %reduce_sum.21, bf16[8192,768]{1,0:T(8,128)(2,1)} %param.3), kind=kOutput, calls=%fused_computation.5 | convolution fusion | flops 805822464 | bytes 12713984 | tf_op jit(solution)/shard_map/dot_general | solution.py:16
  82.9 0.0 copy-start.1
  83.0 151.5 %all-reduce.2.cloned.1.call-done = bf16[8192,768]{1,0:T(8,128)(2,1)} async-done(((bf16[8192,768]{1,0:T(8,128)(2,1)}), bf16[8192,768]{1,0:T(8,128)(2,1)}) %all-reduce.2.cloned.1.call-update) | async-done | bytes 12582928 | tf_op jit(solution)/shard_map/psum | solution.py:31
  234.4 16.8 %maximum_reduce_fusion = f32[1024]{0:T(1024)S(1)} fusion(bf16[8192,768]{1,0:T(8,128)(2,1)} %param.3, f32[8192]{0:T(1024)S(1)} %convolution_reduce_fusion, bf16[8192,768]{1,0:T(8,128)(2,1)} %all-reduce.2.cloned.1.call-done, s32[]{:T(128)S(6)} %select_n.46), kind=kOutput, calls=%fused_computation.2 | convolution fusion | flops 12910066688 | bytes 14192644 | tf_op jit(solution)/shard_map/dot_general | solution.py:16
  251.2 0.0 copy-done.1
  251.3 29.4 %psum.15 = f32[1024]{0:T(1024)S(1)} all-reduce(f32[1024]{0:T(1024)S(1)} %maximum_reduce_fusion), channel_id=1, replica_groups=mesh['row'=16,'cand'=8] {'row'}, use_global_device_ids=true, to_apply=%region_4.5 | all-reduce | flops 1024 | bytes 8192 | tf_op jit(solution)/shard_map/psum | solution.py:39
  280.6 0.6 broadcast_multiply_fusion
  (2 shorter events, 0.0 us)
Async XLA Ops:
  7.2 65.7 %all-gather.2.cloned.1.call-start = ((), (), s32[]{:S(2)}) async-start(), calls=%async_computation.1 | async-start | bytes 1671168 | tf_op jit(solution)/shard_map/all_gather | solution.py:24
  15.6 218.8 %all-reduce.2.cloned.1.call-start = ((), (), s32[]{:S(2)}) async-start(), calls=%async_computation | async-start | bytes 25165824 | tf_op jit(solution)/shard_map/psum | solution.py:31
  16.4 43.3 %copy-start = (s32[8192]{0:T(1024)S(1)}, s32[8192]{0:T(1024)}, u32[]{:S(2)}) copy-start(s32[8192]{0:T(1024)} %param.5) | copy-start | bytes 98308
  82.9 168.3 %copy-start.1 = (f32[8192]{0:T(1024)}, f32[8192]{0:T(1024)S(1)}, u32[]{:S(2)}) copy-start(f32[8192]{0:T(1024)S(1)} %convolution_reduce_fusion) | copy-start | bytes 98308
Sparse Core Ops, SparseCore 0:
  15.7 35.6 all-gather.1
  72.9 161.4 all-reduce.1
